TPU v7x, 512 devices: a whole 4x8x8 slice. The times are simulated.
512 devices in a mesh: grid: 16 (over z, x_hi), recv: 32 (over x_lo, y, core).
Axes of the slice: x: 4 (x_hi: 2, x_lo: 2; x = x_hi * 2 + x_lo), y: 8, z: 8, core: 2. Of those that a mesh axis runs over, the one named last changes fastest.
Arguments:
- spectra: bfloat16 [2, 16, 20480], P(None, 'grid', 'recv'), may hold values from -6 to 6
- library: bfloat16 [16384, 2, 20480], P('grid', None, 'recv'), may hold values from -200 to 200, as said below
Outputs:
- power: float32 [16384], P(('grid', 'recv'))
Inputs may be any that keep to these rules, and one draw needn't show every extreme that they name: `library`: finite values.
All inputs are finite; a program needn't handle non-finite values.
Results may differ from a plain program's by a relative error of at most 0.0003.
Values may be sent and summed in bfloat16 or wider, within the bound.
No kernel may reach another device: no remote copies, remote signals or barrier semaphores. Data moves between devices by JAX's collectives and lax.ppermute only.
A program may use at most 64 MiB of HBM per device.

v0:
```python
import jax
import jax.numpy as jnp
from jax import lax
from jax.sharding import PartitionSpec as P


def shards(spectra, library):
    grid_rows = library.shape[0]
    recv_cols = library.shape[2]
    snap_total = spectra.shape[1] * lax.axis_size("grid")
    flat_lib = library.reshape(grid_rows, 2 * recv_cols)
    piece = lax.all_gather(spectra, "grid", axis=1, tiled=True)
    real_part = piece[0]
    imag_part = piece[1]
    upper = jnp.concatenate([real_part, imag_part], axis=1)
    lower = jnp.concatenate([imag_part, -real_part], axis=1)
    stacked = jnp.concatenate([upper, lower], axis=0)
    product = lax.dot_general(
        stacked, flat_lib, (((1,), (1,)), ((), ())), preferred_element_type=jnp.float32
    )
    partial_value = product.reshape(2, piece.shape[1], grid_rows)
    rows = partial_value.reshape(2 * snap_total, grid_rows)
    wide = library.astype(jnp.float32)
    energy = jnp.sum(wide * wide, axis=(1, 2))
    summed = lax.psum_scatter(rows, "recv", scatter_dimension=1, tiled=True)
    weight = lax.psum_scatter(energy, "recv", scatter_dimension=0, tiled=True)
    total = jnp.sum(summed * summed, axis=0)
    return total / (snap_total * (weight + 1e-06))


def solution(mesh):
    placed = (P(None, "grid", "recv"), P("grid", None, "recv"))
    return jax.shard_map(
        shards, mesh=mesh, in_specs=placed, out_specs=P(("grid", "recv")), check_vma=False
    )
```

profile of v0, /device:TPU:1, one launch (start us, length us, event | category | flops | bytes accessed | tf_op | source)
XLA Modules:
  0.0 177.1 jit_solution(13694396552901170320)
XLA Ops:
  6.5 0.0 reduce-scatter.4.cloned.1.call-start
  6.5 41.1 %all_gather.3 = bf16[2,16,640]{2,0,1:T(2,128)(2,1)S(1)} all-gather(bf16[2,1,640]{2,0,1:T(2,128)(2,1)} %param.2), channel_id=1, replica_groups=mesh['grid'=16,'recv'=32] {'grid'}, dimensions={1}, use_global_device_ids=true | all-gather | bytes 43520 | tf_op jit(solution)/shard_map/all_gather | solution.py:12
  47.6 0.1 fusion.11
  47.7 2.2 %copy.11 = bf16[128,8,2,640]{3,1,2,0:T(8,128)(2,1)S(1)} copy(bf16[128,8,2,640]{3,2,1,0:T(2,128)(2,1)} %bitcast.13) | data formatting | bytes 5242880
  49.9 0.0 copy-start
  49.9 1.6 convolution_bitcast_fusion
  51.5 0.0 reduce-scatter.4.cloned.1.call-update
  51.6 0.1 copy-done
  51.7 4.2 %multiply_reduce_fusion = f32[1024]{0:T(1024)S(1)} fusion(bf16[1024,2,640]{2,1,0:T(2,128)(2,1)S(1)} %copy-done), kind=kLoop, calls=%fused_computation | loop fusion | flops 3931136 | bytes 2625536 | tf_op jit(solution)/shard_map/reduce_sum | solution.py:24
  55.8 1.3 dynamic-slice
  57.8 60.3 %all-reduce = f32[1024]{0:T(1024)S(1)} all-reduce(f32[1024]{0:T(1024)S(1)} %multiply_reduce_fusion), channel_id=3, replica_groups=mesh['grid'=16,'recv'=32] {'recv'}, use_global_device_ids=true, to_apply=%region_3.0.clone | all-reduce | flops 1024 | bytes 8192
  118.0 50.8 %reduce-scatter.4.cloned.1.call-done = f32[32,32]{1,0:T(8,128)} async-done(((f32[1024,32]{1,0:T(8,128)}), f32[32,32]{1,0:T(8,128)}) %reduce-scatter.4.cloned.1.call-update) | async-done | bytes 4112
  168.8 0.8 copy.8
  169.6 0.6 fusion.8
  (3 shorter events, 0.0 us)
Async XLA Ops:
  6.5 162.3 %reduce-scatter.4.cloned.1.call-start = ((), (), s32[]{:S(2)}) async-start(), calls=%async_computation.1 | async-start | bytes 540672
  49.9 1.7 copy-start
Sparse Core Ops, SparseCore 0:
  51.7 117.0 reduce-scatter.3
where the time goes:
time: 179 us; the launch traced here: 177 us
  blocking collectives  101 us (56%)
  waiting for transfers between devices  50.8 us (28%)
  between operations  14.1 us (8%)
  other arithmetic  4.79 us (3%)
  local copies, waits for them, and re-layouts  4.46 us (2%)
    unnamed x1, blocking collectives  60.3 us
    unnamed x2, waiting for transfers between devices  50.8 us
    all_gather x1, blocking collectives, shards(): piece = lax.all_gather(spectra, 'grid', axis=1, tiled=True)  41.1 us
    unnamed x6, local copies, waits for them, and re-layouts  4.4 us
    reduce_sum x1, other arithmetic, shards(): energy = jnp.sum(wide * wide, axis=(1, 2))  4.16 us
  transfers between devices with their start and end apart: 1, of which 1 were waited for; matrix products, arithmetic and copies ran while one was open for 3% of the time, Pallas kernels for 0%

commit v1 on v0

v1 whole, which is shorter than its diff:
```python
import jax
import jax.numpy as jnp
from jax import lax
from jax.sharding import PartitionSpec as P


def shards(spectra, library):
    grid_size = lax.axis_size("grid")
    recv_size = lax.axis_size("recv")
    grid_rows = library.shape[0]
    recv_cols = library.shape[2]
    own_rows = grid_rows // recv_size
    snap_total = spectra.shape[1] * grid_size

    own = spectra.reshape(1, 2, recv_cols)
    piece = lax.all_to_all(
        jnp.broadcast_to(own, (grid_size, 2, recv_cols)), "grid", split_axis=0, concat_axis=0, tiled=True
    )
    real_part = piece[:, 0]
    imag_part = piece[:, 1]
    upper = jnp.concatenate([real_part, imag_part], axis=1)
    lower = jnp.concatenate([imag_part, -real_part], axis=1)
    stacked = jnp.concatenate([upper, lower], axis=0)
    flat_lib = library.reshape(grid_rows, 2 * recv_cols)
    product = lax.dot_general(
        stacked, flat_lib, (((1,), (1,)), ((), ())), preferred_element_type=jnp.float32
    )
    wide = library.astype(jnp.float32)
    energy = jnp.sum(wide * wide, axis=(1, 2))

    rows = jnp.concatenate([product, energy[None]], axis=0)
    blocks = rows.reshape(2 * snap_total + 1, recv_size, own_rows).transpose(1, 0, 2)
    blocks = blocks.reshape(recv_size, 1, (2 * snap_total + 1) * own_rows)
    arrived = lax.all_to_all(blocks, "recv", split_axis=0, concat_axis=0, tiled=True)
    summed = jnp.sum(arrived, axis=(0, 1)).reshape(2 * snap_total + 1, own_rows)
    beams = summed[: 2 * snap_total]
    total = jnp.sum(beams * beams, axis=0)
    weight = summed[2 * snap_total]
    return total / (snap_total * (weight + 1e-06))


def solution(mesh):
    placed = (P(None, "grid", "recv"), P("grid", None, "recv"))
    return jax.shard_map(
        shards, mesh=mesh, in_specs=placed, out_specs=P(("grid", "recv")), check_vma=False
    )
```

time: 179 us -> 47.2 us (0.26)
  blocking collectives: 101 us -> 18.4 us
  waiting for transfers between devices: 50.8 us -> 0.01 us
  between operations: 14.1 us -> 0.08 us
  starting transfers between devices: 0.01 us -> 13.4 us
  other arithmetic: 4.79 us -> 6.79 us
    unnamed x1 -> x0, blocking collectives: 60.3 us -> none
    unnamed x2 -> x0, waiting for transfers between devices: 50.8 us -> none
    all_gather x1 -> x0, blocking collectives: 41.1 us -> none  [shards(): piece = lax.all_gather(spectra, 'grid', axis=1, tiled=True)]
    all_to_all x0 -> x1, blocking collectives: none -> 18.4 us  [shards(): lax.all_to_all(blocks, 'recv', split_axis=0, concat_axis=0, tiled=True)]
    all_to_all x0 -> x1, starting transfers between devices: none -> 13.4 us  [shards(): lax.all_to_all(jnp.broadcast_to(own, (grid_size, 2, recv_cols)), 'grid',...]
    unnamed x6 -> x3, local copies, waits for them, and re-layouts: 4.4 us -> 0.01 us
    dot_general x0 -> x1, local copies, waits for them, and re-layouts: none -> 2.98 us  [shards(): lax.dot_general(stacked, flat_lib, (((1,), (1,)), ((), ())), preferred_el...]
    dot_general x0 -> x1, matrix products: none -> 2.54 us  [shards(): lax.dot_general(stacked, flat_lib, (((1,), (1,)), ((), ())), preferred_el...]
  transfers between devices with their start and end apart: 1 -> 1, of which waited for: 1 -> 0; matrix products, arithmetic and copies ran while one was open for 3% -> 20% of each run, Pallas kernels for 0% -> 0%
where the time goes in v1:
time: 47.2 us; the launch traced here: 46.8 us
  blocking collectives  18.4 us (39%)
  starting transfers between devices  13.4 us (28%)
  other arithmetic  6.79 us (14%)
  local copies, waits for them, and re-layouts  5.51 us (12%)
  matrix products  2.54 us (5%)
    all_to_all x1, blocking collectives, shards(): lax.all_to_all(blocks, 'recv', split_axis=0, concat_axis=0, tiled=True)  18.4 us
    all_to_all x1, starting transfers between devices, shards(): lax.all_to_all(jnp.broadcast_to(own, (grid_size, 2, recv_cols)), 'grid',...  13.4 us
    reduce_sum x1, other arithmetic, shards(): energy = jnp.sum(wide * wide, axis=(1, 2))  5.91 us
    dot_general x1, local copies, waits for them, and re-layouts, shards(): lax.dot_general(stacked, flat_lib, (((1,), (1,)), ((), ())), preferred_el...  2.98 us
    dot_general x1, matrix products, shards(): lax.dot_general(stacked, flat_lib, (((1,), (1,)), ((), ())), preferred_el...  2.54 us
    broadcast_in_dim x1, local copies, waits for them, and re-layouts, shards(): jnp.broadcast_to(own, (grid_size, 2, recv_cols))  1.46 us
  transfers between devices with their start and end apart: 1, of which 0 were waited for; matrix products, arithmetic and copies ran while one was open for 20% of the time, Pallas kernels for 0%

profile of v1, /device:TPU:1, one launch (start us, length us, event | category | flops | bytes accessed | tf_op | source)
XLA Modules:
  0.0 46.8 jit_solution(13478256752666657768)
XLA Ops:
  0.0 0.0 copy-start
  0.0 1.5 %broadcast_in_dim.9 = bf16[16,2,640]{2,1,0:T(2,128)(2,1)} broadcast(bf16[2,640]{1,0:T(2,128)(2,1)} %bitcast.14), dimensions={1,2} | broadcast | bytes 43520 | tf_op jit(solution)/shard_map/broadcast_in_dim | solution.py:17
  1.5 13.4 %all-to-all-start = ((bf16[16,2,640]{2,1,0:T(2,128)(2,1)}), bf16[16,2,640]{2,1,0:T(2,128)(2,1)S(1)}, u32[]{:S(2)}, u32[]{:S(2)}) async-start(bf16[16,2,640]{2,1,0:T(2,128)(2,1)} %broadcast_in_dim.9), calls=%async_computation | async-start | bytes 81920 | tf_op jit(solution)/shard_map/all_to_all | solution.py:16
  14.9 5.9 %multiply_reduce_fusion = f32[1024]{0:T(1024)S(1)} fusion(bf16[1024,2,640]{2,1,0:T(2,128)(2,1)} %param.3), kind=kLoop, calls=%fused_computation | loop fusion | flops 3931136 | bytes 2625536 | tf_op jit(solution)/shard_map/reduce_sum | solution.py:29
  20.8 0.0 copy-done
  20.8 3.0 %dot_general.5 = bf16[32,32,1280]{2,1,0:T(8,128)(2,1)} reshape(bf16[1024,2,640]{2,1,0:T(2,128)(2,1)S(1)} %copy-done) | data formatting | bytes 5242880 | tf_op jit(solution)/shard_map/dot_general | solution.py:25
  23.8 0.3 concatenate.20
  24.1 0.0 all-to-all-done
  24.2 0.1 fusion.11
  24.3 2.5 %fusion = f32[32,32,32]{0,2,1:T(8,128)S(1)} fusion(bf16[32,32,1280]{2,1,0:T(8,128)(2,1)} %dot_general.5, bf16[16,640]{1,0:T(8,128)(2,1)S(1)} %get-tuple-element.5, bf16[16,640]{1,0:T(8,128)(2,1)S(1)} %bitcast.13, bf16[16,640]{1,0:T(8,128)(2,1)S(1)} %get-tuple-element.6), kind=kOutput, calls=%fused_computation.3 | convolution fusion | flops 84213760 | bytes 2813952 | tf_op jit(solution)/shard_map/dot_general | solution.py:25
  26.8 0.2 maximum_bitcast_fusion
  27.0 0.3 copy.13
  27.3 0.3 reshape.27
  27.6 18.4 %all_to_all.10 = f32[32,1,1056]{2,1,0:T(1,128)S(1)} all-to-all(f32[32,1,1056]{2,1,0:T(1,128)S(1)} %reshape.27), channel_id=1, replica_groups=mesh['grid'=16,'recv'=32] {'recv'}, dimensions={0} | all-to-all | bytes 270336 | tf_op jit(solution)/shard_map/all_to_all | solution.py:34
  46.0 0.1 reduce_sum.28
  46.2 0.1 mul.17
  46.3 0.5 %fusion.8 = f32[32]{0:T(128)} fusion(f32[32]{0:T(128)S(1)} %reduce_sum.29, f32[1056]{0:T(1024)S(1)} %reduce_sum.28), kind=kLoop, calls=%fused_computation.15 | loop fusion | flops 96 | bytes 384 | tf_op jit(solution)/shard_map/div | solution.py:39
  (4 shorter events, 0.0 us)
Async XLA Ops:
  0.0 20.8 %copy-start = (bf16[1024,2,640]{2,1,0:T(2,128)(2,1)S(1)}, bf16[1024,2,640]{2,1,0:T(2,128)(2,1)}, u32[]{:S(2)}) copy-start(bf16[1024,2,640]{2,1,0:T(2,128)(2,1)} %param.3) | copy-start | bytes 7864324
  1.5 22.7 %all-to-all-start = ((bf16[16,2,640]{2,1,0:T(2,128)(2,1)}), bf16[16,2,640]{2,1,0:T(2,128)(2,1)S(1)}, u32[]{:S(2)}, u32[]{:S(2)}) async-start(bf16[16,2,640]{2,1,0:T(2,128)(2,1)} %broadcast_in_dim.9), calls=%async_computation | async-start | bytes 81920 | tf_op jit(solution)/shard_map/all_to_all | solution.py:16

commit v2 on v1

v2 whole, which is shorter than its diff:
```python
import functools

import jax
import jax.numpy as jnp
from jax import lax
from jax.experimental import pallas as pl
from jax.experimental.pallas import tpu as pltpu
from jax.sharding import PartitionSpec as P

LANES = 128
SUB = 8
CHUNKS = 8
VMEM = pl.BlockSpec(memory_space=pltpu.VMEM)
PARAMS = pltpu.CompilerParams(vmem_limit_bytes=32 << 20)
NT = (((1,), (1,)), ((), ()))


def pieces(values):
    high = values.astype(jnp.bfloat16)
    rest = values - high.astype(jnp.float32)
    middle = rest.astype(jnp.bfloat16)
    low = (rest - middle.astype(jnp.float32)).astype(jnp.bfloat16)
    return high, middle, low


def split_kernel(lib_hbm, rows_ref, energy_ref, lib_ref, folded_ref, sems):
    owners, parts, sub, _, cols = lib_ref.shape
    tall = 2 * sub
    chunks = sems.shape[0]
    step = owners // chunks
    copies = [
        pltpu.make_async_copy(
            lib_hbm.at[pl.ds(chunk * step, step)], lib_ref.at[pl.ds(chunk * step, step)], sems.at[chunk]
        )
        for chunk in range(chunks)
    ]
    for copy in copies:
        copy.start()
    for chunk in range(chunks):
        copies[chunk].wait()
        for owner in range(chunk * step, (chunk + 1) * step):
            for part in range(parts):
                both = lib_ref[owner, part].reshape(tall, cols)
                rows_ref[part, owner * tall : (owner + 1) * tall, :] = both
                wide = both.astype(jnp.float32)
                square = wide * wide
                folded = square[:, :LANES]
                for start in range(LANES, cols, LANES):
                    folded = folded + square[:, start : start + LANES]
                folded_ref[part, owner * tall : (owner + 1) * tall, :] = folded
    target = lax.broadcasted_iota(jnp.int32, (LANES, LANES), 1)
    found = None
    for part in range(parts):
        ones = ((target >= part * sub) & (target < (part + 1) * sub)).astype(jnp.bfloat16)
        for piece in pieces(folded_ref[part]):
            term = jnp.dot(piece, ones, preferred_element_type=jnp.float32)
            found = term if found is None else found + term
    found = found.reshape(owners, tall, LANES)
    lane = lax.broadcasted_iota(jnp.int32, found.shape, 2)
    row = lax.broadcasted_iota(jnp.int32, found.shape, 1)
    energy_ref[...] = jnp.sum(jnp.where(lane % sub == row // 2, found, 0.0), axis=1)


def beam_kernel(spectra_ref, rows_ref, energy_ref, out_ref):
    parts, height, _ = rows_ref.shape
    tall = 2 * SUB
    owners = height // tall
    real = spectra_ref[:, 0, :]
    imag = spectra_ref[:, 1, :]
    with_real = jnp.concatenate([real, imag], axis=0)
    with_imag = jnp.concatenate([imag, -real], axis=0)
    zero = jnp.zeros_like(with_real)
    total = None
    for part in range(parts):
        placed = jnp.concatenate(
            [half if k == part else zero for half in (with_real, with_imag) for k in range(parts)], axis=0
        )
        term = lax.dot_general(rows_ref[part], placed, NT, preferred_element_type=jnp.float32)
        total = term if total is None else total + term
    even = lax.broadcasted_iota(jnp.int32, (SUB, LANES), 0) % 2 == 0
    for owner in range(owners):
        first = total[owner * tall : owner * tall + SUB]
        second = total[owner * tall + SUB : (owner + 1) * tall]
        of_real = jnp.where(even, first[:, :LANES], pltpu.roll(second[:, :LANES], 1, 0))
        of_imag = jnp.where(even, pltpu.roll(first[:, LANES:], SUB - 1, 0), second[:, LANES:])
        base = owner * (SUB + 1)
        out_ref[base : base + SUB, 0, :] = of_real + of_imag
        out_ref[base + SUB : base + SUB + 1, 0, :] = energy_ref[owner : owner + 1, :]


def power_kernel(snaps, arrived_ref, out_ref):
    height = SUB + 1
    senders = arrived_ref.shape[0] // height
    width = out_ref.shape[1] // SUB
    beams = arrived_ref[0:SUB, 0, :]
    weight = arrived_ref[SUB:height, 0, :]
    for sender in range(1, senders):
        base = sender * height
        beams = beams + arrived_ref[base : base + SUB, 0, :]
        weight = weight + arrived_ref[base + SUB : base + height, 0, :]
    source = lax.broadcasted_iota(jnp.int32, (LANES, LANES), 0)
    target = lax.broadcasted_iota(jnp.int32, (LANES, LANES), 1)
    same = (source // (LANES // width) == target // SUB).astype(jnp.bfloat16)
    stacked = jnp.concatenate(pieces(beams * beams), axis=0)
    found = jnp.dot(stacked, same, preferred_element_type=jnp.float32)
    found = found[:SUB] + found[SUB : 2 * SUB] + found[2 * SUB :]
    lane = lax.broadcasted_iota(jnp.int32, found.shape, 1)
    row = lax.broadcasted_iota(jnp.int32, found.shape, 0)
    point = (row // 2) + (row % 2) * (SUB // 2)
    total = jnp.sum(jnp.where(lane % SUB == point, found, 0.0), axis=0, keepdims=True)
    power = total / (snaps * (weight + 1e-06))
    out_ref[...] = power[:, : out_ref.shape[1]]


def shards(spectra, library):
    grid_size = lax.axis_size("grid")
    recv_size = lax.axis_size("recv")
    grid_rows = library.shape[0]
    recv_cols = library.shape[2]
    own_rows = grid_rows // recv_size
    snap_total = spectra.shape[1] * grid_size
    parts = own_rows // SUB
    height = SUB + 1

    own = spectra.reshape(1, 2, recv_cols)
    piece = lax.all_to_all(
        jnp.broadcast_to(own, (grid_size, 2, recv_cols)), "grid", split_axis=0, concat_axis=0, tiled=True
    )
    rows, energy = pl.pallas_call(
        split_kernel,
        out_shape=(
            jax.ShapeDtypeStruct((parts, recv_size * 2 * SUB, recv_cols), library.dtype),
            jax.ShapeDtypeStruct((recv_size, LANES), jnp.float32),
        ),
        in_specs=[pl.BlockSpec(memory_space=pltpu.HBM)],
        out_specs=(VMEM, VMEM),
        scratch_shapes=[
            pltpu.VMEM((recv_size, parts, SUB, 2, recv_cols), library.dtype),
            pltpu.VMEM((parts, recv_size * 2 * SUB, LANES), jnp.float32),
            pltpu.SemaphoreType.DMA((CHUNKS,)),
        ],
        compiler_params=PARAMS,
        cost_estimate=pl.CostEstimate(flops=4 * library.size, bytes_accessed=4 * library.size, transcendentals=0),
        name="split_rows",
    )(pltpu.with_memory_space_constraint(library.reshape(recv_size, parts, SUB, 2, recv_cols), pltpu.HBM))
    blocks = pl.pallas_call(
        beam_kernel,
        out_shape=jax.ShapeDtypeStruct((recv_size * height, 1, LANES), jnp.float32),
        in_specs=[VMEM, VMEM, VMEM],
        out_specs=VMEM,
        compiler_params=PARAMS,
        cost_estimate=pl.CostEstimate(
            flops=2 * library.size * 2 * snap_total, bytes_accessed=2 * library.size, transcendentals=0
        ),
        name="beams",
    )(piece, rows, energy)
    arrived = lax.all_to_all(blocks, "recv", split_axis=0, concat_axis=0, tiled=True)
    power = pl.pallas_call(
        functools.partial(power_kernel, snap_total),
        out_shape=jax.ShapeDtypeStruct((1, own_rows), jnp.float32),
        in_specs=[VMEM],
        out_specs=VMEM,
        compiler_params=PARAMS,
        name="power",
    )(arrived)
    return power.reshape(own_rows)


def solution(mesh):
    placed = (P(None, "grid", "recv"), P("grid", None, "recv"))
    return jax.shard_map(
        shards, mesh=mesh, in_specs=placed, out_specs=P(("grid", "recv")), check_vma=False
    )
```

time: 47.2 us -> 44.5 us (0.943)
  other arithmetic: 6.79 us -> 0 us
  waiting for transfers between devices: 0.01 us -> 5.54 us
  Pallas kernels: 0 us -> 5.43 us
  local copies, waits for them, and re-layouts: 5.51 us -> 1.32 us
  matrix products: 2.54 us -> 0 us
    reduce_sum x3 -> x0, other arithmetic: 6.04 us -> none  [the longest x1 5.91 us: shards(): energy = jnp.sum(wide * wide, axis=(1, 2))]
    all_to_all x1, waiting for transfers between devices: 0.01 us -> 5.54 us  [shards(): lax.all_to_all(jnp.broadcast_to(own, (grid_size, 2, recv_cols)), 'grid',...]
    pallas_call x0 -> x3, Pallas kernels: none -> 5.43 us  [the longest x1 3.64 us: shards(): pl.pallas_call(split_kernel, out_shape=(jax.ShapeDtypeStruct((parts, recv...]
    dot_general x1 -> x0, local copies, waits for them, and re-layouts: 2.98 us -> none  [shards(): lax.dot_general(stacked, flat_lib, (((1,), (1,)), ((), ())), preferred_el...]
    dot_general x1 -> x0, matrix products: 2.54 us -> none  [shards(): lax.dot_general(stacked, flat_lib, (((1,), (1,)), ((), ())), preferred_el...]
    div x1 -> x0, other arithmetic: 0.53 us -> none  [shards(): return total / (snap_total * (weight + 1e-06))]
  transfers between devices with their start and end apart: 1 -> 1, of which waited for: 0 -> 1; matrix products, arithmetic and copies ran while one was open for 20% -> 0% of each run, Pallas kernels for 0% -> 8%
where the time goes in v2:
time: 44.5 us; the launch traced here: 44.2 us
  blocking collectives  18.5 us (42%)
  starting transfers between devices  13.4 us (30%)
  waiting for transfers between devices  5.54 us (12%)
  Pallas kernels  5.43 us (12%)
  local copies, waits for them, and re-layouts  1.32 us (3%)
    all_to_all x1, blocking collectives, shards(): lax.all_to_all(blocks, 'recv', split_axis=0, concat_axis=0, tiled=True)  18.5 us
    all_to_all x1, starting transfers between devices, shards(): lax.all_to_all(jnp.broadcast_to(own, (grid_size, 2, recv_cols)), 'grid',...  13.4 us
    all_to_all x1, waiting for transfers between devices, shards(): lax.all_to_all(jnp.broadcast_to(own, (grid_size, 2, recv_cols)), 'grid',...  5.54 us
    pallas_call x1, Pallas kernels, shards(): pl.pallas_call(split_kernel, out_shape=(jax.ShapeDtypeStruct((parts, recv...  3.64 us
    broadcast_in_dim x1, local copies, waits for them, and re-layouts, shards(): jnp.broadcast_to(own, (grid_size, 2, recv_cols))  1.32 us
    pallas_call x1, Pallas kernels, shards(): pl.pallas_call(beam_kernel, out_shape=jax.ShapeDtypeStruct((recv_size * h...  1.09 us
  transfers between devices with their start and end apart: 1, of which 1 were waited for; matrix products, arithmetic and copies ran while one was open for 0% of the time, Pallas kernels for 8%

profile of v2, /device:TPU:1, one launch (start us, length us, event | category | flops | bytes accessed | tf_op | source)
XLA Modules:
  0.0 44.2 jit_solution(16051707223483817533)
XLA Ops:
  0.0 1.3 %broadcast_in_dim.8 = bf16[16,2,640]{2,1,0:T(2,128)(2,1)} broadcast(bf16[2,640]{1,0:T(2,128)(2,1)} %bitcast.4), dimensions={1,2} | broadcast | bytes 43520 | tf_op jit(solution)/shard_map/broadcast_in_dim | solution.py:127
  1.3 13.4 %all-to-all-start = ((bf16[16,2,640]{2,1,0:T(2,128)(2,1)}), bf16[16,2,640]{2,1,0:T(2,128)(2,1)S(1)}, u32[]{:S(2)}, u32[]{:S(2)}) async-start(bf16[16,2,640]{2,1,0:T(2,128)(2,1)} %broadcast_in_dim.8), calls=%async_computation | async-start | bytes 81920 | tf_op jit(solution)/shard_map/all_to_all | solution.py:126
  14.8 3.6 %split_rows.1 = (bf16[4,512,640]{2,1,0:T(8,128)(2,1)S(1)}, f32[32,128]{1,0:T(8,128)S(1)}) custom-call(bf16[32,4,8,2,640]{4,3,2,1,0:T(2,128)(2,1)} %bitcast.3), custom_call_target="tpu_custom_call" | custom-call | flops 5242880 | bytes 5242880 | tf_op jit(solution)/shard_map/split_rows/pallas_call | solution.py:129
  18.4 5.5 %all-to-all-done.spectra_ref = bf16[16,2,640]{2,1,0:T(2,128)(2,1)S(1)} async-done(((bf16[16,2,640]{2,1,0:T(2,128)(2,1)}), bf16[16,2,640]{2,1,0:T(2,128)(2,1)S(1)}, u32[]{:S(2)}, u32[]{:S(2)}) %all-to-all-start) | async-done | bytes 40992 | tf_op jit(solution)/shard_map/all_to_all | solution.py:126
  23.9 1.1 %beams.1 = f32[288,1,128]{2,1,0:T(1,128)S(1)} custom-call(bf16[16,2,640]{2,1,0:T(2,128)(2,1)S(1)} %all-to-all-done.spectra_ref, bf16[4,512,640]{2,1,0:T(8,128)(2,1)S(1)} %get-tuple-element.7.rows_ref, f32[32,128]{1,0:T(8,128)S(1)} %get-tuple-element.8.energy_ref), custom_call_target="tpu_custom_call" | custom-call | flops 83886080 | bytes 2621440 | tf_op jit(solution)/shard_map/beams/pallas_call | solution.py:146
  25.0 18.5 %all_to_all.10.arrived_ref = f32[288,1,128]{2,1,0:T(1,128)S(1)} all-to-all(f32[288,1,128]{2,1,0:T(1,128)S(1)} %beams.1), channel_id=1, replica_groups=mesh['grid'=16,'recv'=32] {'recv'}, dimensions={0} | all-to-all | bytes 294912 | tf_op jit(solution)/shard_map/all_to_all | solution.py:157
  43.5 0.7 %power.1 = f32[1,32]{1,0:T(1,128)} custom-call(f32[288,1,128]{2,1,0:T(1,128)S(1)} %all_to_all.10.arrived_ref), custom_call_target="tpu_custom_call" | custom-call | tf_op jit(solution)/shard_map/power/pallas_call | solution.py:158
Async XLA Ops:
  1.3 22.6 %all-to-all-start = ((bf16[16,2,640]{2,1,0:T(2,128)(2,1)}), bf16[16,2,640]{2,1,0:T(2,128)(2,1)S(1)}, u32[]{:S(2)}, u32[]{:S(2)}) async-start(bf16[16,2,640]{2,1,0:T(2,128)(2,1)} %broadcast_in_dim.8), calls=%async_computation | async-start | bytes 81920 | tf_op jit(solution)/shard_map/all_to_all | solution.py:126

commit v3 on v2

--- a/solution.py
+++ b/solution.py
@@ -10,6 +10,7 @@
 LANES = 128
 SUB = 8
 CHUNKS = 8
+EARLY = 6
 VMEM = pl.BlockSpec(memory_space=pltpu.VMEM)
 PARAMS = pltpu.CompilerParams(vmem_limit_bytes=32 << 20)
 NT = (((1,), (1,)), ((), ()))
@@ -23,7 +24,7 @@
     return high, middle, low
 
 
-def split_kernel(lib_hbm, rows_ref, energy_ref, lib_ref, folded_ref, sems):
+def split_rows(slots, lib_hbm, rows_ref, energy_ref, lib_ref, folded_ref, sems):
     owners, parts, sub, _, cols = lib_ref.shape
     tall = 2 * sub
     chunks = sems.shape[0]
@@ -39,15 +40,16 @@
     for chunk in range(chunks):
         copies[chunk].wait()
         for owner in range(chunk * step, (chunk + 1) * step):
+            base = slots[owner] * tall
             for part in range(parts):
                 both = lib_ref[owner, part].reshape(tall, cols)
-                rows_ref[part, owner * tall : (owner + 1) * tall, :] = both
+                rows_ref[part, base : base + tall, :] = both
                 wide = both.astype(jnp.float32)
                 square = wide * wide
                 folded = square[:, :LANES]
                 for start in range(LANES, cols, LANES):
                     folded = folded + square[:, start : start + LANES]
-                folded_ref[part, owner * tall : (owner + 1) * tall, :] = folded
+                folded_ref[part, base : base + tall, :] = folded
     target = lax.broadcasted_iota(jnp.int32, (LANES, LANES), 1)
     found = None
     for part in range(parts):
@@ -61,7 +63,24 @@
     energy_ref[...] = jnp.sum(jnp.where(lane % sub == row // 2, found, 0.0), axis=1)
 
 
-def beam_kernel(spectra_ref, rows_ref, energy_ref, out_ref):
+def leaves_early():
+    return lax.axis_index("grid") < EARLY
+
+
+def prepare_kernel(slots, own_hbm, lib_hbm, out_ref, rows_ref, energy_ref, own_ref, lib_ref, folded_ref, sems, own_sem):
+    copy = pltpu.make_async_copy(own_hbm, own_ref, own_sem)
+    copy.start()
+    copy.wait()
+    own = own_ref[...]
+    for target in range(out_ref.shape[0]):
+        out_ref[target] = own
+
+    @pl.when(leaves_early())
+    def _():
+        split_rows(slots, lib_hbm, rows_ref, energy_ref, lib_ref, folded_ref, sems)
+
+
+def beams(spectra_ref, rows_ref, energy_ref, out_ref):
     parts, height, _ = rows_ref.shape
     tall = 2 * SUB
     owners = height // tall
@@ -88,6 +107,21 @@
         out_ref[base + SUB : base + SUB + 1, 0, :] = energy_ref[owner : owner + 1, :]
 
 
+def beam_kernel(
+    slots, spectra_ref, rows_ref, energy_ref, lib_hbm, out_ref, own_rows_ref, own_energy_ref, lib_ref, folded_ref, sems
+):
+    early = leaves_early()
+
+    @pl.when(early)
+    def _():
+        beams(spectra_ref, rows_ref, energy_ref, out_ref)
+
+    @pl.when(jnp.logical_not(early))
+    def _():
+        split_rows(slots, lib_hbm, own_rows_ref, own_energy_ref, lib_ref, folded_ref, sems)
+        beams(spectra_ref, own_rows_ref, own_energy_ref, out_ref)
+
+
 def power_kernel(snaps, arrived_ref, out_ref):
     height = SUB + 1
     senders = arrived_ref.shape[0] // height
@@ -112,6 +146,18 @@
     out_ref[...] = power[:, : out_ref.shape[1]]
 
 
+def exchange_orders(grid_size, recv_size):
+    grid_order = list(range(grid_size))[::-1]
+    line = recv_size // 2
+    recv_order = [
+        half + (pair + line // 2) % line + core
+        for half in range(0, recv_size, line)
+        for pair in range(0, line, 2)
+        for core in (1, 0)
+    ]
+    return grid_order, recv_order
+
+
 def shards(spectra, library):
     grid_size = lax.axis_size("grid")
     recv_size = lax.axis_size("recv")
@@ -121,40 +167,49 @@
     snap_total = spectra.shape[1] * grid_size
     parts = own_rows // SUB
     height = SUB + 1
-
-    own = spectra.reshape(1, 2, recv_cols)
+    grid_order, recv_order = exchange_orders(grid_size, recv_size)
+    slots = [recv_order.index(owner) for owner in range(recv_size)]
+    hbm = pl.BlockSpec(memory_space=pltpu.HBM)
+    rows_shape = (parts, recv_size * 2 * SUB, recv_cols)
+    energy_shape = (recv_size, LANES)
+    scratch = [
+        pltpu.VMEM((recv_size, parts, SUB, 2, recv_cols), library.dtype),
+        pltpu.VMEM((parts, recv_size * 2 * SUB, LANES), jnp.float32),
+        pltpu.SemaphoreType.DMA((CHUNKS,)),
+    ]
+
+    spectra = pltpu.with_memory_space_constraint(spectra.reshape(2, recv_cols), pltpu.HBM)
+    library = pltpu.with_memory_space_constraint(
+        library.reshape(recv_size, parts, SUB, 2, recv_cols), pltpu.HBM
+    )
+    own, rows, energy = pl.pallas_call(
+        functools.partial(prepare_kernel, slots),
+        out_shape=(
+            jax.ShapeDtypeStruct((grid_size, 2, recv_cols), spectra.dtype),
+            jax.ShapeDtypeStruct(rows_shape, library.dtype),
+            jax.ShapeDtypeStruct(energy_shape, jnp.float32),
+        ),
+        in_specs=[hbm, hbm],
+        out_specs=(VMEM, VMEM, VMEM),
+        scratch_shapes=[pltpu.VMEM((2, recv_cols), spectra.dtype), *scratch, pltpu.SemaphoreType.DMA],
+        compiler_params=PARAMS,
+        name="prepare",
+    )(spectra, library)
     piece = lax.all_to_all(
-        jnp.broadcast_to(own, (grid_size, 2, recv_cols)), "grid", split_axis=0, concat_axis=0, tiled=True
-    )
-    rows, energy = pl.pallas_call(
-        split_kernel,
-        out_shape=(
-            jax.ShapeDtypeStruct((parts, recv_size * 2 * SUB, recv_cols), library.dtype),
-            jax.ShapeDtypeStruct((recv_size, LANES), jnp.float32),
-        ),
-        in_specs=[pl.BlockSpec(memory_space=pltpu.HBM)],
-        out_specs=(VMEM, VMEM),
-        scratch_shapes=[
-            pltpu.VMEM((recv_size, parts, SUB, 2, recv_cols), library.dtype),
-            pltpu.VMEM((parts, recv_size * 2 * SUB, LANES), jnp.float32),
-            pltpu.SemaphoreType.DMA((CHUNKS,)),
-        ],
+        own, "grid", split_axis=0, concat_axis=0, tiled=True, axis_index_groups=[grid_order]
+    )
+    blocks = pl.pallas_call(
+        functools.partial(beam_kernel, slots),
+        out_shape=jax.ShapeDtypeStruct((recv_size * height, 1, LANES), jnp.float32),
+        in_specs=[VMEM, VMEM, VMEM, hbm],
+        out_specs=VMEM,
+        scratch_shapes=[pltpu.VMEM(rows_shape, library.dtype), pltpu.VMEM(energy_shape, jnp.float32), *scratch],
         compiler_params=PARAMS,
-        cost_estimate=pl.CostEstimate(flops=4 * library.size, bytes_accessed=4 * library.size, transcendentals=0),
-        name="split_rows",
-    )(pltpu.with_memory_space_constraint(library.reshape(recv_size, parts, SUB, 2, recv_cols), pltpu.HBM))
-    blocks = pl.pallas_call(
-        beam_kernel,
-        out_shape=jax.ShapeDtypeStruct((recv_size * height, 1, LANES), jnp.float32),
-        in_specs=[VMEM, VMEM, VMEM],
-        out_specs=VMEM,
-        compiler_params=PARAMS,
-        cost_estimate=pl.CostEstimate(
-            flops=2 * library.size * 2 * snap_total, bytes_accessed=2 * library.size, transcendentals=0
-        ),
         name="beams",
-    )(piece, rows, energy)
-    arrived = lax.all_to_all(blocks, "recv", split_axis=0, concat_axis=0, tiled=True)
+    )(piece, rows, energy, library)
+    arrived = lax.all_to_all(
+        blocks, "recv", split_axis=0, concat_axis=0, tiled=True, axis_index_groups=[recv_order]
+    )
     power = pl.pallas_call(
         functools.partial(power_kernel, snap_total),
         out_shape=jax.ShapeDtypeStruct((1, own_rows), jnp.float32),

time: 44.5 us -> 37.3 us (0.84)
  starting transfers between devices: 13.4 us -> 0 us
  blocking collectives: 18.5 us -> 30.9 us
  waiting for transfers between devices: 5.54 us -> 0 us
  local copies, waits for them, and re-layouts: 1.32 us -> 0 us
  Pallas kernels: 5.43 us -> 6.2 us
    all_to_all x1 -> x0, starting transfers between devices: 13.4 us -> none  [shards(): lax.all_to_all(jnp.broadcast_to(own, (grid_size, 2, recv_cols)), 'grid',...]
    all_to_all x1 -> x2, blocking collectives: 18.5 us -> 30.9 us  [the longest x1 15.4 us: shards(): lax.all_to_all(blocks, 'recv', split_axis=0, concat_axis=0, tiled=True, a...]
    all_to_all x1 -> x0, waiting for transfers between devices: 5.54 us -> none  [shards(): lax.all_to_all(jnp.broadcast_to(own, (grid_size, 2, recv_cols)), 'grid',...]
    broadcast_in_dim x1 -> x0, local copies, waits for them, and re-layouts: 1.32 us -> none  [shards(): jnp.broadcast_to(own, (grid_size, 2, recv_cols))]
    pallas_call x2, Pallas kernels: 4.72 us -> 5.49 us  [the longest x1 4.32 us: shards(): pl.pallas_call(functools.partial(prepare_kernel, slots), out_shape=(jax.S...]
  transfers between devices with their start and end apart: 1 -> 0, of which waited for: 1 -> 0; matrix products, arithmetic and copies ran while one was open for 0% -> 0% of each run, Pallas kernels for 8% -> 0%
where the time goes in v3:
time: 37.3 us; the launch traced here: 37.1 us
  blocking collectives  30.9 us (83%)
  Pallas kernels  6.2 us (17%)
    all_to_all x1, blocking collectives, shards(): lax.all_to_all(blocks, 'recv', split_axis=0, concat_axis=0, tiled=True, a...  15.4 us
    all_to_all x1, blocking collectives, shards(): lax.all_to_all(own, 'grid', split_axis=0, concat_axis=0, tiled=True, axis...  15.4 us
    pallas_call x1, Pallas kernels, shards(): pl.pallas_call(functools.partial(prepare_kernel, slots), out_shape=(jax.S...  4.32 us
    pallas_call x1, Pallas kernels, shards(): pl.pallas_call(functools.partial(beam_kernel, slots), out_shape=jax.Shape...  1.17 us

profile of v3, /device:TPU:1, one launch (start us, length us, event | category | flops | bytes accessed | tf_op | source)
XLA Modules:
  0.0 37.1 jit_solution(17217197969463832938)
XLA Ops:
  0.0 4.3 %prepare.1 = (bf16[16,2,640]{2,1,0:T(2,128)(2,1)S(1)}, bf16[4,512,640]{2,1,0:T(8,128)(2,1)S(1)}, f32[32,128]{1,0:T(8,128)S(1)}) custom-call(bf16[2,640]{1,0:T(2,128)(2,1)} %bitcast.5, bf16[32,4,8,2,640]{4,3,2,1,0:T(2,128)(2,1)} %bitcast.3), custom_call_target="tpu_custom_call" | custom-call | tf_op jit(solution)/shard_map/prepare/pallas_call | solution.py:185
  4.3 15.4 %all_to_all.10.spectra_ref = bf16[16,2,640]{2,1,0:T(2,128)(2,1)S(1)} all-to-all(bf16[16,2,640]{2,1,0:T(2,128)(2,1)S(1)} %get-tuple-element.8), channel_id=1, replica_groups={{480,448,416,384,352,320,288,256,224,192,160,128,96,64,32,0},{481,449,4..., dimensions={0} | all-to-all | bytes 81920 | tf_op jit(solution)/shard_map/all_to_all | solution.py:198
  19.8 1.2 %beams.1 = f32[288,1,128]{2,1,0:T(1,128)S(1)} custom-call(bf16[16,2,640]{2,1,0:T(2,128)(2,1)S(1)} %all_to_all.10.spectra_ref, bf16[4,512,640]{2,1,0:T(8,128)(2,1)S(1)} %get-tuple-element.9.rows_ref, f32[32,128]{1,0:T(8,128)S(1)} %get-tuple-element.10.energy_ref, bf16[32,4,8,2,640]{4,3,2,1,0:T(2,128)(2,1)} %bitcast.4), custom_call_target="tpu_custom_call" | custom-call | tf_op jit(solution)/shard_map/beams/pallas_call | solution.py:201
  20.9 15.4 %all_to_all.11.arrived_ref = f32[288,1,128]{2,1,0:T(1,128)S(1)} all-to-all(f32[288,1,128]{2,1,0:T(1,128)S(1)} %beams.1), channel_id=1, replica_groups={{9,8,11,10,13,12,15,14,1,0,3,2,5,4,7,6,25,24,27,26,29,28,31,30,17,16,19..., dimensions={0} | all-to-all | bytes 294912 | tf_op jit(solution)/shard_map/all_to_all | solution.py:210
  36.4 0.7 %power.1 = f32[1,32]{1,0:T(1,128)} custom-call(f32[288,1,128]{2,1,0:T(1,128)S(1)} %all_to_all.11.arrived_ref), custom_call_target="tpu_custom_call" | custom-call | tf_op jit(solution)/shard_map/power/pallas_call | solution.py:213

commit v4 on v3

--- a/solution.py
+++ b/solution.py
@@ -43,7 +43,8 @@
             base = slots[owner] * tall
             for part in range(parts):
                 both = lib_ref[owner, part].reshape(tall, cols)
-                rows_ref[part, base : base + tall, :] = both
+                side = part % 2 * cols
+                rows_ref[part // 2, base : base + tall, side : side + cols] = both
                 wide = both.astype(jnp.float32)
                 square = wide * wide
                 folded = square[:, :LANES]
@@ -72,8 +73,10 @@
     copy.start()
     copy.wait()
     own = own_ref[...]
-    for target in range(out_ref.shape[0]):
-        out_ref[target] = own
+    tiles = own.shape[1] // LANES
+    for target in range(out_ref.shape[0] // tiles):
+        for tile in range(tiles):
+            out_ref[target * tiles + tile] = own[:, tile * LANES : (tile + 1) * LANES]
 
     @pl.when(leaves_early())
     def _():
@@ -81,20 +84,28 @@
 
 
 def beams(spectra_ref, rows_ref, energy_ref, out_ref):
-    parts, height, _ = rows_ref.shape
+    pairs, height, _ = rows_ref.shape
+    parts = 2 * pairs
     tall = 2 * SUB
     owners = height // tall
-    real = spectra_ref[:, 0, :]
-    imag = spectra_ref[:, 1, :]
+    tiles = rows_ref.shape[2] // (2 * LANES)
+    snaps = spectra_ref.shape[0] // tiles
+    by_tile = [spectra_ref[pl.ds(tile, snaps, stride=tiles)] for tile in range(tiles)]
+    real = jnp.concatenate([block[:, 0, :] for block in by_tile], axis=1)
+    imag = jnp.concatenate([block[:, 1, :] for block in by_tile], axis=1)
     with_real = jnp.concatenate([real, imag], axis=0)
     with_imag = jnp.concatenate([imag, -real], axis=0)
     zero = jnp.zeros_like(with_real)
-    total = None
-    for part in range(parts):
-        placed = jnp.concatenate(
+
+    def placed(part):
+        return jnp.concatenate(
             [half if k == part else zero for half in (with_real, with_imag) for k in range(parts)], axis=0
         )
-        term = lax.dot_general(rows_ref[part], placed, NT, preferred_element_type=jnp.float32)
+
+    total = None
+    for pair in range(pairs):
+        weights = jnp.concatenate([placed(2 * pair), placed(2 * pair + 1)], axis=1)
+        term = lax.dot_general(rows_ref[pair], weights, NT, preferred_element_type=jnp.float32)
         total = term if total is None else total + term
     even = lax.broadcasted_iota(jnp.int32, (SUB, LANES), 0) % 2 == 0
     for owner in range(owners):
@@ -170,7 +181,7 @@
     grid_order, recv_order = exchange_orders(grid_size, recv_size)
     slots = [recv_order.index(owner) for owner in range(recv_size)]
     hbm = pl.BlockSpec(memory_space=pltpu.HBM)
-    rows_shape = (parts, recv_size * 2 * SUB, recv_cols)
+    rows_shape = (parts // 2, recv_size * 2 * SUB, 2 * recv_cols)
     energy_shape = (recv_size, LANES)
     scratch = [
         pltpu.VMEM((recv_size, parts, SUB, 2, recv_cols), library.dtype),
@@ -185,7 +196,7 @@
     own, rows, energy = pl.pallas_call(
         functools.partial(prepare_kernel, slots),
         out_shape=(
-            jax.ShapeDtypeStruct((grid_size, 2, recv_cols), spectra.dtype),
+            jax.ShapeDtypeStruct((grid_size * (recv_cols // LANES), 2, LANES), spectra.dtype),
             jax.ShapeDtypeStruct(rows_shape, library.dtype),
             jax.ShapeDtypeStruct(energy_shape, jnp.float32),
         ),

time: 37.3 us -> 37.1 us (level)
  no operation moved by 1% of the time
where the time goes in v4:
time: 37.1 us; the launch traced here: 36.9 us
  blocking collectives  30.9 us (83%)
  Pallas kernels  5.99 us (16%)
    all_to_all x1, blocking collectives, shards(): lax.all_to_all(blocks, 'recv', split_axis=0, concat_axis=0, tiled=True, a...  15.5 us
    all_to_all x1, blocking collectives, shards(): lax.all_to_all(own, 'grid', split_axis=0, concat_axis=0, tiled=True, axis...  15.4 us
    pallas_call x1, Pallas kernels, shards(): pl.pallas_call(functools.partial(prepare_kernel, slots), out_shape=(jax.S...  4.34 us
    pallas_call x1, Pallas kernels, shards(): pl.pallas_call(functools.partial(beam_kernel, slots), out_shape=jax.Shape...  0.94 us

profile of v4, /device:TPU:1, one launch (start us, length us, event | category | flops | bytes accessed | tf_op | source)
XLA Modules:
  0.0 36.9 jit_solution(3545462477366643883)
XLA Ops:
  0.0 4.3 %prepare.1 = (bf16[80,2,128]{2,1,0:T(2,128)(2,1)S(1)}, bf16[2,512,1280]{2,1,0:T(8,128)(2,1)S(1)}, f32[32,128]{1,0:T(8,128)S(1)}) custom-call(bf16[2,640]{1,0:T(2,128)(2,1)} %bitcast.5, bf16[32,4,8,2,640]{4,3,2,1,0:T(2,128)(2,1)} %bitcast.3), custom_call_target="tpu_custom_call" | custom-call | tf_op jit(solution)/shard_map/prepare/pallas_call | solution.py:196
  4.3 15.4 %all_to_all.10.spectra_ref = bf16[80,2,128]{2,1,0:T(2,128)(2,1)S(1)} all-to-all(bf16[80,2,128]{2,1,0:T(2,128)(2,1)S(1)} %get-tuple-element.8), channel_id=1, replica_groups={{480,448,416,384,352,320,288,256,224,192,160,128,96,64,32,0},{481,449,4..., dimensions={0} | all-to-all | bytes 81920 | tf_op jit(solution)/shard_map/all_to_all | solution.py:209
  19.8 0.9 %beams.1 = f32[288,1,128]{2,1,0:T(1,128)S(1)} custom-call(bf16[80,2,128]{2,1,0:T(2,128)(2,1)S(1)} %all_to_all.10.spectra_ref, bf16[2,512,1280]{2,1,0:T(8,128)(2,1)S(1)} %get-tuple-element.9.rows_ref, f32[32,128]{1,0:T(8,128)S(1)} %get-tuple-element.10.energy_ref, bf16[32,4,8,2,640]{4,3,2,1,0:T(2,128)(2,1)} %bitcast.4), custom_call_target="tpu_custom_call" | custom-call | tf_op jit(solution)/shard_map/beams/pallas_call | solution.py:212
  20.7 15.5 %all_to_all.11.arrived_ref = f32[288,1,128]{2,1,0:T(1,128)S(1)} all-to-all(f32[288,1,128]{2,1,0:T(1,128)S(1)} %beams.1), channel_id=1, replica_groups={{9,8,11,10,13,12,15,14,1,0,3,2,5,4,7,6,25,24,27,26,29,28,31,30,17,16,19..., dimensions={0} | all-to-all | bytes 294912 | tf_op jit(solution)/shard_map/all_to_all | solution.py:221
  36.2 0.7 %power.1 = f32[1,32]{1,0:T(1,128)} custom-call(f32[288,1,128]{2,1,0:T(1,128)S(1)} %all_to_all.11.arrived_ref), custom_call_target="tpu_custom_call" | custom-call | tf_op jit(solution)/shard_map/power/pallas_call | solution.py:224

commit v5 on v4

--- a/solution.py
+++ b/solution.py
@@ -11,6 +11,10 @@
 SUB = 8
 CHUNKS = 8
 EARLY = 6
+WIDTH = 32
+BLOCK = 5
+TOP = 15
+LOWEST = -14
 VMEM = pl.BlockSpec(memory_space=pltpu.VMEM)
 PARAMS = pltpu.CompilerParams(vmem_limit_bytes=32 << 20)
 NT = (((1,), (1,)), ((), ()))
@@ -24,7 +28,33 @@
     return high, middle, low
 
 
-def split_rows(slots, lib_hbm, rows_ref, energy_ref, lib_ref, folded_ref, sems):
+def exponent(squares, highest):
+    half = 0.5 * jnp.log2(jnp.maximum(squares, 1e-30)) + 0.01
+    return jnp.clip(jnp.ceil(half), LOWEST, highest)
+
+
+def point_of(row):
+    return row // 2 + row % 2 * (SUB // 2)
+
+
+def widen(points, first):
+    owners = points.shape[0]
+    shape = (owners, SUB, LANES)
+    lane = lax.broadcasted_iota(jnp.int32, shape, 2)
+    row = lax.broadcasted_iota(jnp.int32, shape, 1)
+    own = (lane >= first) & (lane < first + WIDTH) & (lane % SUB == point_of(row))
+    spread = jnp.where(own, jnp.broadcast_to(points[:, None, :], shape), 0.0)
+    source = lax.broadcasted_iota(jnp.int32, (LANES, LANES), 0)
+    target = lax.broadcasted_iota(jnp.int32, (LANES, LANES), 1)
+    same = ((source - first) // SUB == target // WIDTH) & (source >= first)
+    return jnp.dot(
+        spread.reshape(owners * SUB, LANES).astype(jnp.bfloat16),
+        same.astype(jnp.bfloat16),
+        preferred_element_type=jnp.float32,
+    )
+
+
+def split_rows(slots, lib_hbm, rows_ref, tail_ref, lift_ref, lib_ref, folded_ref, sems):
     owners, parts, sub, _, cols = lib_ref.shape
     tall = 2 * sub
     chunks = sems.shape[0]
@@ -61,14 +91,22 @@
     found = found.reshape(owners, tall, LANES)
     lane = lax.broadcasted_iota(jnp.int32, found.shape, 2)
     row = lax.broadcasted_iota(jnp.int32, found.shape, 1)
-    energy_ref[...] = jnp.sum(jnp.where(lane % sub == row // 2, found, 0.0), axis=1)
+    energy = jnp.sum(jnp.where(lane % sub == row // 2, found, 0.0), axis=1)
+    power = exponent(energy, 13)
+    high, middle, low = pieces(jnp.sqrt(energy))
+    lane = lax.broadcasted_iota(jnp.int32, energy.shape, 1)
+    tail = jnp.where(lane < WIDTH, high.astype(jnp.float32), pltpu.roll(jnp.exp2(power), 3 * WIDTH, 1))
+    tail = jnp.where(lane // WIDTH == 1, pltpu.roll(middle.astype(jnp.float32) * 2.0**8, WIDTH, 1), tail)
+    tail = jnp.where(lane // WIDTH == 2, pltpu.roll(low.astype(jnp.float32) * 2.0**16, 2 * WIDTH, 1), tail)
+    tail_ref[...] = tail
+    lift_ref[...] = widen(jnp.exp2(TOP - power), 0)
 
 
 def leaves_early():
     return lax.axis_index("grid") < EARLY
 
 
-def prepare_kernel(slots, own_hbm, lib_hbm, out_ref, rows_ref, energy_ref, own_ref, lib_ref, folded_ref, sems, own_sem):
+def prepare_kernel(slots, own_hbm, lib_hbm, out_ref, rows_ref, tail_ref, lift_ref, own_ref, lib_ref, folded_ref, sems, own_sem):
     copy = pltpu.make_async_copy(own_hbm, own_ref, own_sem)
     copy.start()
     copy.wait()
@@ -80,10 +118,10 @@
 
     @pl.when(leaves_early())
     def _():
-        split_rows(slots, lib_hbm, rows_ref, energy_ref, lib_ref, folded_ref, sems)
-
-
-def beams(spectra_ref, rows_ref, energy_ref, out_ref):
+        split_rows(slots, lib_hbm, rows_ref, tail_ref, lift_ref, lib_ref, folded_ref, sems)
+
+
+def beams(spectra_ref, rows_ref, tail_ref, lift_ref, out_ref):
     pairs, height, _ = rows_ref.shape
     parts = 2 * pairs
     tall = 2 * SUB
@@ -94,6 +132,11 @@
     real = jnp.concatenate([block[:, 0, :] for block in by_tile], axis=1)
     imag = jnp.concatenate([block[:, 1, :] for block in by_tile], axis=1)
     with_real = jnp.concatenate([real, imag], axis=0)
+    wide = with_real.astype(jnp.float32)
+    squares = jnp.sum(jnp.sum(wide * wide, axis=0, keepdims=True), axis=1, keepdims=True)
+    power = exponent(squares, 10)
+    inverse = jnp.exp2(-power)
+    scale = jnp.broadcast_to(jnp.exp2(power), (1, LANES))
     with_imag = jnp.concatenate([imag, -real], axis=0)
     zero = jnp.zeros_like(with_real)
 
@@ -113,36 +156,42 @@
         second = total[owner * tall + SUB : (owner + 1) * tall]
         of_real = jnp.where(even, first[:, :LANES], pltpu.roll(second[:, :LANES], 1, 0))
         of_imag = jnp.where(even, pltpu.roll(first[:, LANES:], SUB - 1, 0), second[:, LANES:])
-        base = owner * (SUB + 1)
-        out_ref[base : base + SUB, 0, :] = of_real + of_imag
-        out_ref[base + SUB : base + SUB + 1, 0, :] = energy_ref[owner : owner + 1, :]
+        scaled = (of_real + of_imag) * (lift_ref[owner * SUB : (owner + 1) * SUB] * inverse)
+        base = owner * BLOCK
+        for pair in range(SUB // 2):
+            out_ref[base + pair] = scaled[2 * pair : 2 * pair + 2]
+        out_ref[base + SUB // 2, 0:1, :] = tail_ref[owner : owner + 1]
+        out_ref[base + SUB // 2, 1:2, :] = scale
 
 
 def beam_kernel(
-    slots, spectra_ref, rows_ref, energy_ref, lib_hbm, out_ref, own_rows_ref, own_energy_ref, lib_ref, folded_ref, sems
+    slots, spectra_ref, rows_ref, tail_ref, lift_ref, lib_hbm, out_ref, own_rows, own_tail, own_lift, lib_ref, folded_ref, sems
 ):
     early = leaves_early()
 
     @pl.when(early)
     def _():
-        beams(spectra_ref, rows_ref, energy_ref, out_ref)
+        beams(spectra_ref, rows_ref, tail_ref, lift_ref, out_ref)
 
     @pl.when(jnp.logical_not(early))
     def _():
-        split_rows(slots, lib_hbm, own_rows_ref, own_energy_ref, lib_ref, folded_ref, sems)
-        beams(spectra_ref, own_rows_ref, own_energy_ref, out_ref)
+        split_rows(slots, lib_hbm, own_rows, own_tail, own_lift, lib_ref, folded_ref, sems)
+        beams(spectra_ref, own_rows, own_tail, own_lift, out_ref)
 
 
 def power_kernel(snaps, arrived_ref, out_ref):
-    height = SUB + 1
-    senders = arrived_ref.shape[0] // height
+    senders = arrived_ref.shape[0] // BLOCK
     width = out_ref.shape[1] // SUB
-    beams = arrived_ref[0:SUB, 0, :]
-    weight = arrived_ref[SUB:height, 0, :]
-    for sender in range(1, senders):
-        base = sender * height
-        beams = beams + arrived_ref[base : base + SUB, 0, :]
-        weight = weight + arrived_ref[base + SUB : base + height, 0, :]
+    tail = arrived_ref[pl.ds(SUB // 2, senders, stride=BLOCK), 0, :]
+    scale = arrived_ref[pl.ds(SUB // 2, senders, stride=BLOCK), 1, :] * 2.0**-TOP
+    root = tail + pltpu.roll(tail, 3 * WIDTH, 1) * 2.0**-8 + pltpu.roll(tail, 2 * WIDTH, 1) * 2.0**-16
+    weight = jnp.sum(root * root, axis=0, keepdims=True)
+    factor = widen(tail, 3 * WIDTH)
+    beams = None
+    for sender in range(senders):
+        block = arrived_ref[sender * BLOCK : sender * BLOCK + SUB // 2].reshape(SUB, LANES)
+        own = block * (factor[sender * SUB : (sender + 1) * SUB] * scale[sender : sender + 1])
+        beams = own if beams is None else beams + own
     source = lax.broadcasted_iota(jnp.int32, (LANES, LANES), 0)
     target = lax.broadcasted_iota(jnp.int32, (LANES, LANES), 1)
     same = (source // (LANES // width) == target // SUB).astype(jnp.bfloat16)
@@ -151,7 +200,7 @@
     found = found[:SUB] + found[SUB : 2 * SUB] + found[2 * SUB :]
     lane = lax.broadcasted_iota(jnp.int32, found.shape, 1)
     row = lax.broadcasted_iota(jnp.int32, found.shape, 0)
-    point = (row // 2) + (row % 2) * (SUB // 2)
+    point = point_of(row)
     total = jnp.sum(jnp.where(lane % SUB == point, found, 0.0), axis=0, keepdims=True)
     power = total / (snaps * (weight + 1e-06))
     out_ref[...] = power[:, : out_ref.shape[1]]
@@ -177,12 +226,12 @@
     own_rows = grid_rows // recv_size
     snap_total = spectra.shape[1] * grid_size
     parts = own_rows // SUB
-    height = SUB + 1
     grid_order, recv_order = exchange_orders(grid_size, recv_size)
     slots = [recv_order.index(owner) for owner in range(recv_size)]
     hbm = pl.BlockSpec(memory_space=pltpu.HBM)
     rows_shape = (parts // 2, recv_size * 2 * SUB, 2 * recv_cols)
-    energy_shape = (recv_size, LANES)
+    tail_shape = (recv_size, LANES)
+    lift_shape = (recv_size * SUB, LANES)
     scratch = [
         pltpu.VMEM((recv_size, parts, SUB, 2, recv_cols), library.dtype),
         pltpu.VMEM((parts, recv_size * 2 * SUB, LANES), jnp.float32),
@@ -193,15 +242,16 @@
     library = pltpu.with_memory_space_constraint(
         library.reshape(recv_size, parts, SUB, 2, recv_cols), pltpu.HBM
     )
-    own, rows, energy = pl.pallas_call(
+    own, rows, tail, lift = pl.pallas_call(
         functools.partial(prepare_kernel, slots),
         out_shape=(
             jax.ShapeDtypeStruct((grid_size * (recv_cols // LANES), 2, LANES), spectra.dtype),
             jax.ShapeDtypeStruct(rows_shape, library.dtype),
-            jax.ShapeDtypeStruct(energy_shape, jnp.float32),
+            jax.ShapeDtypeStruct(tail_shape, jnp.float32),
+            jax.ShapeDtypeStruct(lift_shape, jnp.float32),
         ),
         in_specs=[hbm, hbm],
-        out_specs=(VMEM, VMEM, VMEM),
+        out_specs=(VMEM, VMEM, VMEM, VMEM),
         scratch_shapes=[pltpu.VMEM((2, recv_cols), spectra.dtype), *scratch, pltpu.SemaphoreType.DMA],
         compiler_params=PARAMS,
         name="prepare",
@@ -211,15 +261,15 @@
     )
     blocks = pl.pallas_call(
         functools.partial(beam_kernel, slots),
-        out_shape=jax.ShapeDtypeStruct((recv_size * height, 1, LANES), jnp.float32),
-        in_specs=[VMEM, VMEM, VMEM, hbm],
+        out_shape=jax.ShapeDtypeStruct((recv_size * BLOCK, 2, LANES), jnp.float32),
+        in_specs=[VMEM, VMEM, VMEM, VMEM, hbm],
         out_specs=VMEM,
-        scratch_shapes=[pltpu.VMEM(rows_shape, library.dtype), pltpu.VMEM(energy_shape, jnp.float32), *scratch],
+        scratch_shapes=[pltpu.VMEM(rows_shape, library.dtype), pltpu.VMEM(tail_shape, jnp.float32), pltpu.VMEM(lift_shape, jnp.float32), *scratch],
         compiler_params=PARAMS,
         name="beams",
-    )(piece, rows, energy, library)
+    )(piece, rows, tail, lift, library)
     arrived = lax.all_to_all(
-        blocks, "recv", split_axis=0, concat_axis=0, tiled=True, axis_index_groups=[recv_order]
+        blocks.astype(jnp.float16), "recv", split_axis=0, concat_axis=0, tiled=True, axis_index_groups=[recv_order]
     )
     power = pl.pallas_call(
         functools.partial(power_kernel, snap_total),
@@ -228,7 +278,7 @@
         out_specs=VMEM,
         compiler_params=PARAMS,
         name="power",
-    )(arrived)
+    )(arrived.astype(jnp.float32))
     return power.reshape(own_rows)
 
 

time: 37.1 us -> 36.3 us (0.978)
  blocking collectives: 30.9 us -> 29.6 us
  Pallas kernels: 5.99 us -> 6.38 us
    all_to_all x1, blocking collectives: 15.5 us -> 14.4 us  [shards(): lax.all_to_all(blocks.astype(jnp.float16), 'recv', split_axis=0, concat_a...]
where the time goes in v5:
time: 36.3 us; the launch traced here: 36.1 us
  blocking collectives  29.6 us (82%)
  Pallas kernels  6.38 us (18%)
    all_to_all x1, blocking collectives, shards(): lax.all_to_all(own, 'grid', split_axis=0, concat_axis=0, tiled=True, axis...  15.2 us
    all_to_all x1, blocking collectives, shards(): lax.all_to_all(blocks.astype(jnp.float16), 'recv', split_axis=0, concat_a...  14.4 us
    pallas_call x1, Pallas kernels, shards(): pl.pallas_call(functools.partial(prepare_kernel, slots), out_shape=(jax.S...  4.58 us
    pallas_call x1, Pallas kernels, shards(): pl.pallas_call(functools.partial(beam_kernel, slots), out_shape=jax.Shape...  0.94 us
    pallas_call x1, Pallas kernels, shards(): pl.pallas_call(functools.partial(power_kernel, snap_total), out_shape=jax...  0.86 us

profile of v5, /device:TPU:1, one launch (start us, length us, event | category | flops | bytes accessed | tf_op | source)
XLA Modules:
  0.0 36.1 jit_solution(13488350946716713171)
XLA Ops:
  0.0 4.6 %prepare.1 = (bf16[80,2,128]{2,1,0:T(2,128)(2,1)S(1)}, bf16[2,512,1280]{2,1,0:T(8,128)(2,1)S(1)}, f32[32,128]{1,0:T(8,128)S(1)}, f32[256,128]{1,0:T(8,128)S(1)}) custom-call(bf16[2,640]{1,0:T(2,128)(2,1)} %bitcast.5, bf16[32,4,8,2,640]{4,3,2,1,0:T(2,128)(2,1)} %bitcast.3), custom_call_target="tpu_custom_call" | custom-call | tf_op jit(solution)/shard_map/prepare/pallas_call | solution.py:245
  4.6 15.2 %all_to_all.10.spectra_ref = bf16[80,2,128]{2,1,0:T(2,128)(2,1)S(1)} all-to-all(bf16[80,2,128]{2,1,0:T(2,128)(2,1)S(1)} %get-tuple-element.9), channel_id=1, replica_groups={{480,448,416,384,352,320,288,256,224,192,160,128,96,64,32,0},{481,449,4..., dimensions={0} | all-to-all | bytes 81920 | tf_op jit(solution)/shard_map/all_to_all | solution.py:259
  19.8 0.9 %beams.1 = f32[160,2,128]{2,1,0:T(2,128)S(1)} custom-call(bf16[80,2,128]{2,1,0:T(2,128)(2,1)S(1)} %all_to_all.10.spectra_ref, bf16[2,512,1280]{2,1,0:T(8,128)(2,1)S(1)} %get-tuple-element.10.rows_ref, f32[32,128]{1,0:T(8,128)S(1)} %get-tuple-element.11.tail_ref, f32[256,128]{1,0:T(8,128)S(1)} %get-tuple-element.12.lift_ref, bf16[32,4,8,2,640]{4,3,2,1,0:T(2,128)(2,1)} %bitcast.4), custom_call_target="tpu_custom_call" | custom-call | tf_op jit(solution)/shard_map/beams/pallas_call | solution.py:262
  20.7 0.1 convert_element_type.6
  20.8 14.4 %all_to_all.11 = f16[160,2,128]{2,1,0:T(2,128)(2,1)S(1)} all-to-all(f16[160,2,128]{2,1,0:T(2,128)(2,1)S(1)} %convert_element_type.6), channel_id=1, replica_groups={{9,8,11,10,13,12,15,14,1,0,3,2,5,4,7,6,25,24,27,26,29,28,31,30,17,16,19..., dimensions={0} | all-to-all | bytes 163840 | tf_op jit(solution)/shard_map/all_to_all | solution.py:271
  35.2 0.1 convert_element_type.7.arrived_ref
  35.2 0.9 %power.1 = f32[1,32]{1,0:T(1,128)} custom-call(f32[160,2,128]{2,1,0:T(2,128)S(1)} %convert_element_type.7.arrived_ref), custom_call_target="tpu_custom_call" | custom-call | tf_op jit(solution)/shard_map/power/pallas_call | solution.py:274

commit v6 on v5

--- a/solution.py
+++ b/solution.py
@@ -209,12 +209,16 @@
 def exchange_orders(grid_size, recv_size):
     grid_order = list(range(grid_size))[::-1]
     line = recv_size // 2
+    ring = line // 2
     recv_order = [
-        half + (pair + line // 2) % line + core
-        for half in range(0, recv_size, line)
-        for pair in range(0, line, 2)
+        half + 2 * pair + core
+        for pair in sorted(range(ring), key=lambda pair: min(pair, ring - pair))
+        for half in (0, line)
         for core in (1, 0)
     ]
+    last = line + 2 * (ring // 2) + 1
+    recv_order.remove(last)
+    recv_order.insert(0, last)
     return grid_order, recv_order
 
 

time: 36.3 us -> 36.2 us (level)
  no operation moved by 1% of the time
where the time goes in v6:
time: 36.2 us; the launch traced here: 36 us
  blocking collectives  29.5 us (81%)
  Pallas kernels  6.33 us (17%)
    all_to_all x1, blocking collectives, shards(): lax.all_to_all(own, 'grid', split_axis=0, concat_axis=0, tiled=True, axis...  15.2 us
    all_to_all x1, blocking collectives, shards(): lax.all_to_all(blocks.astype(jnp.float16), 'recv', split_axis=0, concat_a...  14.3 us
    pallas_call x1, Pallas kernels, shards(): pl.pallas_call(functools.partial(prepare_kernel, slots), out_shape=(jax.S...  4.54 us
    pallas_call x1, Pallas kernels, shards(): pl.pallas_call(functools.partial(beam_kernel, slots), out_shape=jax.Shape...  0.94 us
    pallas_call x1, Pallas kernels, shards(): pl.pallas_call(functools.partial(power_kernel, snap_total), out_shape=jax...  0.86 us

profile of v6, /device:TPU:1, one launch (start us, length us, event | category | flops | bytes accessed | tf_op | source)
XLA Modules:
  0.0 36.0 jit_solution(7152870716759970371)
XLA Ops:
  0.0 4.5 %prepare.1 = (bf16[80,2,128]{2,1,0:T(2,128)(2,1)S(1)}, bf16[2,512,1280]{2,1,0:T(8,128)(2,1)S(1)}, f32[32,128]{1,0:T(8,128)S(1)}, f32[256,128]{1,0:T(8,128)S(1)}) custom-call(bf16[2,640]{1,0:T(2,128)(2,1)} %bitcast.5, bf16[32,4,8,2,640]{4,3,2,1,0:T(2,128)(2,1)} %bitcast.3), custom_call_target="tpu_custom_call" | custom-call | tf_op jit(solution)/shard_map/prepare/pallas_call | solution.py:249
  4.5 15.2 %all_to_all.10.spectra_ref = bf16[80,2,128]{2,1,0:T(2,128)(2,1)S(1)} all-to-all(bf16[80,2,128]{2,1,0:T(2,128)(2,1)S(1)} %get-tuple-element.9), channel_id=1, replica_groups={{480,448,416,384,352,320,288,256,224,192,160,128,96,64,32,0},{481,449,4..., dimensions={0} | all-to-all | bytes 81920 | tf_op jit(solution)/shard_map/all_to_all | solution.py:263
  19.8 0.9 %beams.1 = f32[160,2,128]{2,1,0:T(2,128)S(1)} custom-call(bf16[80,2,128]{2,1,0:T(2,128)(2,1)S(1)} %all_to_all.10.spectra_ref, bf16[2,512,1280]{2,1,0:T(8,128)(2,1)S(1)} %get-tuple-element.10.rows_ref, f32[32,128]{1,0:T(8,128)S(1)} %get-tuple-element.11.tail_ref, f32[256,128]{1,0:T(8,128)S(1)} %get-tuple-element.12.lift_ref, bf16[32,4,8,2,640]{4,3,2,1,0:T(2,128)(2,1)} %bitcast.4), custom_call_target="tpu_custom_call" | custom-call | tf_op jit(solution)/shard_map/beams/pallas_call | solution.py:266
  20.7 0.1 convert_element_type.6
  20.8 14.3 %all_to_all.11 = f16[160,2,128]{2,1,0:T(2,128)(2,1)S(1)} all-to-all(f16[160,2,128]{2,1,0:T(2,128)(2,1)S(1)} %convert_element_type.6), channel_id=1, replica_groups={{25,1,0,17,16,3,2,19,18,15,14,31,30,5,4,21,20,13,12,29,28,7,6,23,22,11,..., dimensions={0} | all-to-all | bytes 163840 | tf_op jit(solution)/shard_map/all_to_all | solution.py:275
  35.1 0.1 convert_element_type.7.arrived_ref
  35.1 0.9 %power.1 = f32[1,32]{1,0:T(1,128)} custom-call(f32[160,2,128]{2,1,0:T(2,128)S(1)} %convert_element_type.7.arrived_ref), custom_call_target="tpu_custom_call" | custom-call | tf_op jit(solution)/shard_map/power/pallas_call | solution.py:278

commit v7 on v6

--- a/solution.py
+++ b/solution.py
@@ -186,11 +186,11 @@
     scale = arrived_ref[pl.ds(SUB // 2, senders, stride=BLOCK), 1, :] * 2.0**-TOP
     root = tail + pltpu.roll(tail, 3 * WIDTH, 1) * 2.0**-8 + pltpu.roll(tail, 2 * WIDTH, 1) * 2.0**-16
     weight = jnp.sum(root * root, axis=0, keepdims=True)
-    factor = widen(tail, 3 * WIDTH)
+    factor = widen(tail * scale, 3 * WIDTH)
     beams = None
     for sender in range(senders):
         block = arrived_ref[sender * BLOCK : sender * BLOCK + SUB // 2].reshape(SUB, LANES)
-        own = block * (factor[sender * SUB : (sender + 1) * SUB] * scale[sender : sender + 1])
+        own = block * factor[sender * SUB : (sender + 1) * SUB]
         beams = own if beams is None else beams + own
     source = lax.broadcasted_iota(jnp.int32, (LANES, LANES), 0)
     target = lax.broadcasted_iota(jnp.int32, (LANES, LANES), 1)

time: 36.2 us -> 36.2 us (level)
  no operation moved by 1% of the time
where the time goes in v7:
time: 36.2 us; the launch traced here: 36 us
  blocking collectives  29.5 us (81%)
  Pallas kernels  6.33 us (17%)
    all_to_all x1, blocking collectives, shards(): lax.all_to_all(own, 'grid', split_axis=0, concat_axis=0, tiled=True, axis...  15.2 us
    all_to_all x1, blocking collectives, shards(): lax.all_to_all(blocks.astype(jnp.float16), 'recv', split_axis=0, concat_a...  14.3 us
    pallas_call x1, Pallas kernels, shards(): pl.pallas_call(functools.partial(prepare_kernel, slots), out_shape=(jax.S...  4.54 us
    pallas_call x1, Pallas kernels, shards(): pl.pallas_call(functools.partial(beam_kernel, slots), out_shape=jax.Shape...  0.94 us
    pallas_call x1, Pallas kernels, shards(): pl.pallas_call(functools.partial(power_kernel, snap_total), out_shape=jax...  0.85 us

profile of v7, /device:TPU:1, one launch (start us, length us, event | category | flops | bytes accessed | tf_op | source)
XLA Modules:
  0.0 36.0 jit_solution(1243234485818680101)
XLA Ops:
  0.0 4.5 %prepare.1 = (bf16[80,2,128]{2,1,0:T(2,128)(2,1)S(1)}, bf16[2,512,1280]{2,1,0:T(8,128)(2,1)S(1)}, f32[32,128]{1,0:T(8,128)S(1)}, f32[256,128]{1,0:T(8,128)S(1)}) custom-call(bf16[2,640]{1,0:T(2,128)(2,1)} %bitcast.5, bf16[32,4,8,2,640]{4,3,2,1,0:T(2,128)(2,1)} %bitcast.3), custom_call_target="tpu_custom_call" | custom-call | tf_op jit(solution)/shard_map/prepare/pallas_call | solution.py:249
  4.5 15.2 %all_to_all.10.spectra_ref = bf16[80,2,128]{2,1,0:T(2,128)(2,1)S(1)} all-to-all(bf16[80,2,128]{2,1,0:T(2,128)(2,1)S(1)} %get-tuple-element.9), channel_id=1, replica_groups={{480,448,416,384,352,320,288,256,224,192,160,128,96,64,32,0},{481,449,4..., dimensions={0} | all-to-all | bytes 81920 | tf_op jit(solution)/shard_map/all_to_all | solution.py:263
  19.8 0.9 %beams.1 = f32[160,2,128]{2,1,0:T(2,128)S(1)} custom-call(bf16[80,2,128]{2,1,0:T(2,128)(2,1)S(1)} %all_to_all.10.spectra_ref, bf16[2,512,1280]{2,1,0:T(8,128)(2,1)S(1)} %get-tuple-element.10.rows_ref, f32[32,128]{1,0:T(8,128)S(1)} %get-tuple-element.11.tail_ref, f32[256,128]{1,0:T(8,128)S(1)} %get-tuple-element.12.lift_ref, bf16[32,4,8,2,640]{4,3,2,1,0:T(2,128)(2,1)} %bitcast.4), custom_call_target="tpu_custom_call" | custom-call | tf_op jit(solution)/shard_map/beams/pallas_call | solution.py:266
  20.7 0.1 convert_element_type.6
  20.8 14.3 %all_to_all.11 = f16[160,2,128]{2,1,0:T(2,128)(2,1)S(1)} all-to-all(f16[160,2,128]{2,1,0:T(2,128)(2,1)S(1)} %convert_element_type.6), channel_id=1, replica_groups={{25,1,0,17,16,3,2,19,18,15,14,31,30,5,4,21,20,13,12,29,28,7,6,23,22,11,..., dimensions={0} | all-to-all | bytes 163840 | tf_op jit(solution)/shard_map/all_to_all | solution.py:275
  35.1 0.1 convert_element_type.7.arrived_ref
  35.1 0.9 %power.1 = f32[1,32]{1,0:T(1,128)} custom-call(f32[160,2,128]{2,1,0:T(2,128)S(1)} %convert_element_type.7.arrived_ref), custom_call_target="tpu_custom_call" | custom-call | tf_op jit(solution)/shard_map/power/pallas_call | solution.py:278

commit v8 on v6

--- a/solution.py
+++ b/solution.py
@@ -207,7 +207,7 @@
 
 
 def exchange_orders(grid_size, recv_size):
-    grid_order = list(range(grid_size))[::-1]
+    grid_order = [grid_size - 3, *(place for place in range(grid_size)[::-1] if place != grid_size - 3)]
     line = recv_size // 2
     ring = line // 2
     recv_order = [

time: 36.2 us -> 36.2 us (level)
  no operation moved by 1% of the time
where the time goes in v8:
time: 36.2 us; the launch traced here: 36 us
  blocking collectives  29.5 us (81%)
  Pallas kernels  6.35 us (18%)
    all_to_all x1, blocking collectives, shards(): lax.all_to_all(own, 'grid', split_axis=0, concat_axis=0, tiled=True, axis...  15.2 us
    all_to_all x1, blocking collectives, shards(): lax.all_to_all(blocks.astype(jnp.float16), 'recv', split_axis=0, concat_a...  14.3 us
    pallas_call x1, Pallas kernels, shards(): pl.pallas_call(functools.partial(prepare_kernel, slots), out_shape=(jax.S...  4.54 us
    pallas_call x1, Pallas kernels, shards(): pl.pallas_call(functools.partial(beam_kernel, slots), out_shape=jax.Shape...  0.95 us
    pallas_call x1, Pallas kernels, shards(): pl.pallas_call(functools.partial(power_kernel, snap_total), out_shape=jax...  0.86 us

profile of v8, /device:TPU:1, one launch (start us, length us, event | category | flops | bytes accessed | tf_op | source)
XLA Modules:
  0.0 36.0 jit_solution(9632129350195285079)
XLA Ops:
  0.0 4.5 %prepare.1 = (bf16[80,2,128]{2,1,0:T(2,128)(2,1)S(1)}, bf16[2,512,1280]{2,1,0:T(8,128)(2,1)S(1)}, f32[32,128]{1,0:T(8,128)S(1)}, f32[256,128]{1,0:T(8,128)S(1)}) custom-call(bf16[2,640]{1,0:T(2,128)(2,1)} %bitcast.5, bf16[32,4,8,2,640]{4,3,2,1,0:T(2,128)(2,1)} %bitcast.3), custom_call_target="tpu_custom_call" | custom-call | tf_op jit(solution)/shard_map/prepare/pallas_call | solution.py:249
  4.5 15.2 %all_to_all.10.spectra_ref = bf16[80,2,128]{2,1,0:T(2,128)(2,1)S(1)} all-to-all(bf16[80,2,128]{2,1,0:T(2,128)(2,1)S(1)} %get-tuple-element.9), channel_id=1, replica_groups={{416,480,448,384,352,320,288,256,224,192,160,128,96,64,32,0},{417,481,4..., dimensions={0} | all-to-all | bytes 81920 | tf_op jit(solution)/shard_map/all_to_all | solution.py:263
  19.8 1.0 %beams.1 = f32[160,2,128]{2,1,0:T(2,128)S(1)} custom-call(bf16[80,2,128]{2,1,0:T(2,128)(2,1)S(1)} %all_to_all.10.spectra_ref, bf16[2,512,1280]{2,1,0:T(8,128)(2,1)S(1)} %get-tuple-element.10.rows_ref, f32[32,128]{1,0:T(8,128)S(1)} %get-tuple-element.11.tail_ref, f32[256,128]{1,0:T(8,128)S(1)} %get-tuple-element.12.lift_ref, bf16[32,4,8,2,640]{4,3,2,1,0:T(2,128)(2,1)} %bitcast.4), custom_call_target="tpu_custom_call" | custom-call | tf_op jit(solution)/shard_map/beams/pallas_call | solution.py:266
  20.8 0.1 convert_element_type.6
  20.8 14.3 %all_to_all.11 = f16[160,2,128]{2,1,0:T(2,128)(2,1)S(1)} all-to-all(f16[160,2,128]{2,1,0:T(2,128)(2,1)S(1)} %convert_element_type.6), channel_id=1, replica_groups={{25,1,0,17,16,3,2,19,18,15,14,31,30,5,4,21,20,13,12,29,28,7,6,23,22,11,..., dimensions={0} | all-to-all | bytes 163840 | tf_op jit(solution)/shard_map/all_to_all | solution.py:275
  35.1 0.1 convert_element_type.7.arrived_ref
  35.1 0.9 %power.1 = f32[1,32]{1,0:T(1,128)} custom-call(f32[160,2,128]{2,1,0:T(2,128)S(1)} %convert_element_type.7.arrived_ref), custom_call_target="tpu_custom_call" | custom-call | tf_op jit(solution)/shard_map/power/pallas_call | solution.py:278
